TPU v7x, 32 devices: a whole 2x2x4 slice. The times are simulated.
32 devices in a mesh: row: 4 (over y, x), col: 8 (over z, core).
Axes of the slice: x: 2, y: 2, z: 4, core: 2. Of those that a mesh axis runs over, the one named last changes fastest.
Arguments:
- trail: bfloat16 [1024, 24576], P('row', 'col'), may hold values from -6 to 6
- trail_rows: int32 [16, 192], P('row', 'col'), may hold values from 0 to 47, as said below
- owner_x: bfloat16 [16384, 1024], P(('row', 'col')), may hold values from -0.1875 to 0.1875
- owner_y: bfloat16 [16384, 1024], P(('row', 'col')), may hold values from -6 to 6
- owner_of: int32 [192], replicated, may hold values from 0 to 7, as said below
- inv_first: bfloat16 [2, 256, 256], replicated, may hold values from -0.25 to 0.25
- inv_second: bfloat16 [2, 256, 256], replicated, may hold values from -0.25 to 0.25
- couple_right: bfloat16 [2, 256, 256], replicated, may hold values from -0.25 to 0.25
- couple_left: bfloat16 [2, 256, 256], replicated, may hold values from -0.25 to 0.25
Outputs:
- updated_trail: bfloat16 [1024, 24576], P('row', 'col')
Inputs may be any that keep to these rules, and one draw needn't show every extreme that they name: `trail_rows`: for each grid row and each block column, the 4 entries in rows r * 4 to r * 4 + 3 are distinct local block rows. `owner_of`: the 6 blocks r * 48 + c * 6 + k (k < 6) have distinct owners; one owner holds at most 8 blocks of its grid row, and some owner of every grid row holds exactly 8.
All inputs are finite; a program needn't handle non-finite values.
Results may differ from a plain program's by a relative error of at most 0.0062.
Values may be sent and summed in bfloat16 or wider, within the bound.
A program may use at most 128 MiB of HBM per device.

v0:
```python
import jax
import jax.numpy as jnp
from jax import lax
from jax.sharding import PartitionSpec as P

BS = 64
PANEL = 256
PER = 6


def real_form(pair):
    top_rows = jnp.concatenate([pair[0], pair[1]], axis=1)
    low_rows = jnp.concatenate([-pair[1], pair[0]], axis=1)
    return jnp.concatenate([top_rows, low_rows], axis=0)


def halves(matrix):
    first_half = jnp.concatenate([matrix[:, :PANEL], matrix[:, 2 * PANEL : 3 * PANEL]], axis=1)
    second_half = jnp.concatenate([matrix[:, PANEL : 2 * PANEL], matrix[:, 3 * PANEL :]], axis=1)
    return (first_half, second_half)


def join_panels(left_part, right_part):
    return jnp.concatenate(
        [left_part[:, :PANEL], right_part[:, :PANEL], left_part[:, PANEL:], right_part[:, PANEL:]],
        axis=1,
    )


def form_rows(matrix, inv_first, inv_second, couple_right):
    first_half, second_half = halves(matrix)
    low_first = jnp.dot(
        first_half, real_form(inv_first), preferred_element_type=jnp.float32
    ).astype(jnp.bfloat16)
    remainder = second_half.astype(jnp.float32) - jnp.dot(
        low_first, real_form(couple_right), preferred_element_type=jnp.float32
    )
    remainder = remainder.astype(jnp.bfloat16)
    low_second = jnp.dot(
        remainder, real_form(inv_second), preferred_element_type=jnp.float32
    ).astype(jnp.bfloat16)
    return join_panels(low_first, low_second)


def form_cols(matrix, inv_first, couple_left):
    coupling = jnp.dot(
        jnp.concatenate([couple_left[0], couple_left[1]], axis=1),
        real_form(inv_first),
        preferred_element_type=jnp.float32,
    ).astype(jnp.bfloat16)
    transposed = jnp.stack([coupling[:, :PANEL].T, coupling[:, PANEL:].T])
    first_half, second_half = halves(matrix)
    remainder = second_half.astype(jnp.float32) - jnp.dot(
        first_half, real_form(transposed), preferred_element_type=jnp.float32
    )
    return join_panels(first_half, remainder.astype(jnp.bfloat16))


def stack_cols(upper_rows):
    count = upper_rows.shape[0] // BS
    real_part = upper_rows[:, : 2 * PANEL]
    imag_part = upper_rows[:, 2 * PANEL :]
    top_rows = jnp.concatenate([real_part, -imag_part], axis=1).reshape(count, BS, 4 * PANEL)
    low_rows = jnp.concatenate([imag_part, real_part], axis=1).reshape(count, BS, 4 * PANEL)
    return jnp.concatenate([top_rows, low_rows], axis=1)


def local(
    trail, trail_rows, owner_x, owner_y, owner_of, inv_first, inv_second, couple_right, couple_left
):
    col_count = lax.axis_size("col")
    my_row = lax.axis_index("row")
    my_col = lax.axis_index("col")
    row_width = 4 * PANEL
    row_blocks = PER * col_count
    owners = lax.dynamic_slice_in_dim(owner_of, my_row * row_blocks, row_blocks)
    owner_marks = (owners[:, None] == jnp.arange(col_count, dtype=jnp.int32)[None, :]).astype(
        jnp.int32
    )
    before = jnp.cumsum(owner_marks, axis=0, dtype=jnp.int32) - owner_marks
    slot_index = jnp.sum(before * owner_marks, axis=1, dtype=jnp.int32).reshape(col_count, PER)
    owner_grid = owners.reshape(col_count, PER)
    my_marks = (owner_grid == my_col).astype(jnp.int32)
    send_slots = jnp.sum(my_marks * slot_index, axis=1, dtype=jnp.int32)
    held_x = owner_x.reshape(-1, BS, row_width)
    held_y = owner_y.reshape(-1, BS, row_width)
    got_x, got_y = (
        lax.all_to_all(held_x[send_slots], "col", split_axis=0, concat_axis=0, tiled=True),
        lax.all_to_all(held_y[send_slots], "col", split_axis=0, concat_axis=0, tiled=True),
    )
    sources = lax.dynamic_index_in_dim(owner_grid, my_col, 0, keepdims=False)
    own_x = got_x[sources].reshape(PER * BS, row_width)
    own_y = got_y[sources].reshape(PER * BS, row_width)
    lower_rows = form_rows(
        lax.all_gather(own_x, "col", axis=0, tiled=True), inv_first, inv_second, couple_right
    )
    upper_rows = form_cols(lax.all_gather(own_y, "row", axis=0, tiled=True), inv_first, couple_left)
    stacked = stack_cols(upper_rows)
    column_count = stacked.shape[0]
    lower_blocks = lower_rows.reshape(-1, BS, row_width)
    trail_tiles = trail.reshape(-1, BS, column_count, 2 * BS)

    def one_slot(inputs):
        block_tile, pattern_rows = inputs
        picked = lower_blocks[pattern_rows]
        change = jnp.einsum("jbp,jqp->bjq", picked, stacked, preferred_element_type=jnp.float32)
        return (block_tile.astype(jnp.float32) - change).astype(jnp.bfloat16)

    updated = lax.map(one_slot, (trail_tiles, trail_rows))
    return updated.reshape(trail.shape)


def solution(mesh):
    placed = (
        P("row", "col"),
        P("row", "col"),
        P(("row", "col"), None),
        P(("row", "col"), None),
        P(),
        P(),
        P(),
        P(),
        P(),
    )
    return jax.shard_map(
        local, mesh=mesh, in_specs=placed, out_specs=P("row", "col"), check_vma=False
    )
```

profile of v0, /device:TPU:0, one launch (start us, length us, event | category | flops | bytes accessed | tf_op | source)
XLA Modules:
  0.0 239.3 jit_solution(10763192760506426968)
XLA Ops:
  6.5 0.8 dynamic_slice.15
  8.0 1.6 gather_fusion.3
  9.6 6.3 %all-to-all-start.1 = ((bf16[8,64,1024]{2,1,0:T(8,128)(2,1)}), bf16[8,64,1024]{2,1,0:T(8,128)(2,1)S(1)}, u32[]{:S(2)}, u32[]{:S(2)}) async-start(bf16[8,64,1024]{2,1,0:T(8,128)(2,1)} %gather_fusion.3), calls=%async_computation.1 | async-start | bytes 2097152 | tf_op jit(solution)/shard_map/all_to_all | solution.py:89
  16.0 26.5 %all-to-all-done.1 = bf16[8,64,1024]{2,1,0:T(8,128)(2,1)S(1)} async-done(((bf16[8,64,1024]{2,1,0:T(8,128)(2,1)}), bf16[8,64,1024]{2,1,0:T(8,128)(2,1)S(1)}, u32[]{:S(2)}, u32[]{:S(2)}) %all-to-all-start.1) | async-done | bytes 1048608 | tf_op jit(solution)/shard_map/all_to_all | solution.py:89
  42.5 1.5 gather_fusion.4
  44.1 0.6 gather_fusion.1
  44.8 29.0 %all_to_all.10 = bf16[8,64,1024]{2,1,0:T(8,128)(2,1)S(1)} all-to-all(bf16[8,64,1024]{2,1,0:T(8,128)(2,1)S(1)} %gather_fusion.1), channel_id=1, replica_groups=mesh['row'=4,'col'=8] {'col'}, dimensions={0} | all-to-all | bytes 2097152 | tf_op jit(solution)/shard_map/all_to_all | solution.py:88
  73.8 1.6 gather_fusion.2
  75.4 2.9 %copy.18 = bf16[32,8,24,128]{3,2,1,0:T(8,128)(2,1)} copy(bf16[32,8,24,128]{3,1,2,0:T(8,128)(2,1)} %bitcast.102) | data formatting | bytes 3145728
  78.4 0.3 convolution_convert_fusion.2
  78.8 0.8 slice_bitcast_fusion.4
  79.6 7.5 %all-gather.5.cloned.1.call-done = bf16[1536,1024]{1,0:T(8,128)(2,1)} async-done(((bf16[384,1024]{1,0:T(8,128)(2,1)}), bf16[1536,1024]{1,0:T(8,128)(2,1)}) %all-gather.5.cloned.1.call-update) | async-done | bytes 3145744 | tf_op jit(solution)/shard_map/all_gather | solution.py:97
  87.1 2.1 fusion.54
  89.2 1.0 fusion.8
  90.4 0.3 maximum_negate_fusion
  90.8 0.5 pad_maximum_fusion.2
  91.3 3.1 %pad_maximum_fusion.1 = bf16[24,128,1024]{2,1,0:T(8,128)(2,1)} fusion(bf16[24,64,1024]{2,1,0:T(8,128)(2,1)S(1)} %bitcast.95, bf16[24,64,512]{2,1,0:T(8,128)(2,1)S(1)} %maximum_negate_fusion, bf16[24,64,512]{2,1,0:T(8,128)(2,1)S(1)} %bitcast.99), kind=kLoop, calls=%fused_computation.18 | loop fusion | flops 18874368 | bytes 12582912 | tf_op jit(solution)/shard_map/concatenate | solution.py:65
  94.4 59.1 %all-gather.3.cloned.1.call-done = bf16[3072,1024]{1,0:T(8,128)(2,1)} async-done(((bf16[384,1024]{1,0:T(8,128)(2,1)}), bf16[3072,1024]{1,0:T(8,128)(2,1)}) %all-gather.3.cloned.1.call-update) | async-done | bytes 6291472 | tf_op jit(solution)/shard_map/all_gather | solution.py:95
  153.6 4.9 %fusion.53 = (bf16[3072,256]{1,0:T(8,128)(2,1)}, bf16[3072,256]{1,0:T(8,128)(2,1)}, bf16[3072,256]{1,0:T(8,128)(2,1)S(1)}, bf16[3072,256]{1,0:T(8,128)(2,1)S(1)}) fusion(bf16[3072,1024]{1,0:T(8,128)(2,1)} %all-gather.3.cloned.1.call-done), kind=kLoop, calls=%fused_computation.87 | loop fusion | bytes 12582912 | tf_op jit(solution)/shard_map/slice | solution.py:19
  158.5 1.9 convolution_convert_fusion.1
  160.4 0.2 fusion.55
  160.6 1.5 copy-done.2
  162.1 8.1 %convolution_convert_fusion = bf16[3072,512]{0,1:T(8,128)(2,1)} fusion(bf16[3072,512]{0,1:T(8,128)(2,1)} %copy-done.2, bf16[3072,256]{1,0:T(8,128)(2,1)} %get-tuple-element.63, bf16[3072,256]{1,0:T(8,128)(2,1)} %get-tuple-element.62, bf16[256,256]{1,0:T(8,128)(2,1)} %get-tuple-element.86, bf16[256,256]{1,0:T(8,128)(2,1)S(1)} %get-tuple-element.88, ...), kind=kOutput, calls=%fused_computation.20 | convolution fusion | flops 3236429824 | bytes 10223616 | tf_op jit(solution)/shard_map/dot_general | solution.py:39
  170.2 2.1 fusion.56
  172.3 3.2 %pad_maximum_fusion = bf16[3072,1024]{0,1:T(8,128)(2,1)} fusion(bf16[3072,256]{0,1:T(8,128)(2,1)S(1)} %get-tuple-element.73, bf16[3072,256]{0,1:T(8,128)(2,1)S(1)} %get-tuple-element.71, bf16[3072,256]{0,1:T(8,128)(2,1)S(1)} %get-tuple-element.72, bf16[3072,256]{0,1:T(8,128)(2,1)S(1)} %get-tuple-element.70), kind=kLoop, calls=%fused_computation.17 | loop fusion | flops 25165824 | bytes 12582912 | tf_op jit(solution)/shard_map/concatenate | solution.py:24
  175.5 8.6 %copy.12 = bf16[3072,1024]{1,0:T(8,128)(2,1)} copy(bf16[3072,1024]{0,1:T(8,128)(2,1)} %pad_maximum_fusion) | data formatting | bytes 12582912 | tf_op jit(solution)/shard_map/concatenate | solution.py:24
  184.1 45.4 %while.10 = (s32[]{:T(128)}, bf16[4,64,24,128]{3,2,1,0:T(8,128)(2,1)}, bf16[4,64,24,128]{3,2,1,0:T(8,128)(2,1)}, s32[4,24]{1,0:T(4,128)}, bf16[48,64,1024]{2,1,0...) while((s32[]{:T(128)}, bf16[4,64,24,128]{3,2,1,0:T(8,128)(2,1)}, ...), condition=%wide.region_4.5_spmd, body=%wide.region_3.4_spmd.sunk | while | flops 403244096 | bytes 18093012 | solution.py:109
  184.1 0.7 fusion.67
  184.8 3.5 %gather_fusion = bf16[24,64,1024]{2,1,0:T(8,128)(2,1)S(1)} fusion(bf16[48,64,1024]{2,1,0:T(8,128)(2,1)} %get-tuple-element.145, s32[1024]{0:T(1024)S(1)} %pad_clamp_fusion.4), kind=kCustom, calls=%fused_computation.clone.1 | custom fusion | bytes 6291552 | tf_op jit(solution)/shard_map/while/body/eval_jaxpr/gather | solution.py:105
  188.4 1.0 constant_dynamic-slice_fusion.3
  189.4 5.1 %fusion.68 = bf16[1,64,24,128]{3,1,2,0:T(8,128)(2,1)S(1)} fusion(bf16[24,64,1024]{2,1,0:T(8,128)(2,1)S(1)} %gather_fusion, bf16[24,128,1024]{2,1,0:T(8,128)(2,1)} %get-tuple-element.146, bf16[1,64,24,128]{3,2,1,0:T(8,128)(2,1)S(1)} %constant_dynamic-slice_fusion.3), kind=kOutput, calls=%fused_computation.8.clone.1 | convolution fusion | flops 403243008 | bytes 10223616 | tf_op jit(solution)/shard_map/while/body/eval_jaxpr/jbp,jqp->bjq/dot_general | solution.py:106
  194.5 1.0 copy_dynamic-update-slice_fusion.2
  195.5 0.7 fusion.67
  196.2 3.5 %gather_fusion = bf16[24,64,1024]{2,1,0:T(8,128)(2,1)S(1)} fusion(bf16[48,64,1024]{2,1,0:T(8,128)(2,1)} %get-tuple-element.145, s32[1024]{0:T(1024)S(1)} %pad_clamp_fusion.4), kind=kCustom, calls=%fused_computation.clone.1 | custom fusion | bytes 6291552 | tf_op jit(solution)/shard_map/while/body/eval_jaxpr/gather | solution.py:105
  199.7 1.0 constant_dynamic-slice_fusion.3
  200.8 5.1 %fusion.68 = bf16[1,64,24,128]{3,1,2,0:T(8,128)(2,1)S(1)} fusion(bf16[24,64,1024]{2,1,0:T(8,128)(2,1)S(1)} %gather_fusion, bf16[24,128,1024]{2,1,0:T(8,128)(2,1)} %get-tuple-element.146, bf16[1,64,24,128]{3,2,1,0:T(8,128)(2,1)S(1)} %constant_dynamic-slice_fusion.3), kind=kOutput, calls=%fused_computation.8.clone.1 | convolution fusion | flops 403243008 | bytes 10223616 | tf_op jit(solution)/shard_map/while/body/eval_jaxpr/jbp,jqp->bjq/dot_general | solution.py:106
  205.8 1.0 copy_dynamic-update-slice_fusion.2
  206.8 0.7 fusion.67
  207.5 3.5 %gather_fusion = bf16[24,64,1024]{2,1,0:T(8,128)(2,1)S(1)} fusion(bf16[48,64,1024]{2,1,0:T(8,128)(2,1)} %get-tuple-element.145, s32[1024]{0:T(1024)S(1)} %pad_clamp_fusion.4), kind=kCustom, calls=%fused_computation.clone.1 | custom fusion | bytes 6291552 | tf_op jit(solution)/shard_map/while/body/eval_jaxpr/gather | solution.py:105
  211.1 1.0 constant_dynamic-slice_fusion.3
  212.1 5.1 %fusion.68 = bf16[1,64,24,128]{3,1,2,0:T(8,128)(2,1)S(1)} fusion(bf16[24,64,1024]{2,1,0:T(8,128)(2,1)S(1)} %gather_fusion, bf16[24,128,1024]{2,1,0:T(8,128)(2,1)} %get-tuple-element.146, bf16[1,64,24,128]{3,2,1,0:T(8,128)(2,1)S(1)} %constant_dynamic-slice_fusion.3), kind=kOutput, calls=%fused_computation.8.clone.1 | convolution fusion | flops 403243008 | bytes 10223616 | tf_op jit(solution)/shard_map/while/body/eval_jaxpr/jbp,jqp->bjq/dot_general | solution.py:106
  217.2 1.0 copy_dynamic-update-slice_fusion.2
  218.2 0.7 fusion.67
  218.9 3.5 %gather_fusion = bf16[24,64,1024]{2,1,0:T(8,128)(2,1)S(1)} fusion(bf16[48,64,1024]{2,1,0:T(8,128)(2,1)} %get-tuple-element.145, s32[1024]{0:T(1024)S(1)} %pad_clamp_fusion.4), kind=kCustom, calls=%fused_computation.clone.1 | custom fusion | bytes 6291552 | tf_op jit(solution)/shard_map/while/body/eval_jaxpr/gather | solution.py:105
  222.4 1.0 constant_dynamic-slice_fusion.3
  223.5 5.1 %fusion.68 = bf16[1,64,24,128]{3,1,2,0:T(8,128)(2,1)S(1)} fusion(bf16[24,64,1024]{2,1,0:T(8,128)(2,1)S(1)} %gather_fusion, bf16[24,128,1024]{2,1,0:T(8,128)(2,1)} %get-tuple-element.146, bf16[1,64,24,128]{3,2,1,0:T(8,128)(2,1)S(1)} %constant_dynamic-slice_fusion.3), kind=kOutput, calls=%fused_computation.8.clone.1 | convolution fusion | flops 403243008 | bytes 10223616 | tf_op jit(solution)/shard_map/while/body/eval_jaxpr/jbp,jqp->bjq/dot_general | solution.py:106
  228.5 1.0 copy_dynamic-update-slice_fusion.2
  229.6 3.0 %copy.25 = bf16[32,8,24,128]{3,1,2,0:T(8,128)(2,1)} copy(bf16[32,8,24,128]{3,2,1,0:T(8,128)(2,1)} %bitcast.33) | data formatting | bytes 3145728
  (42 shorter events, 1.1 us)
Async XLA Ops:
  6.5 1.5 copy-start
  8.0 36.1 %copy-start.3 = (bf16[512,1024]{1,0:T(8,128)(2,1)S(1)}, bf16[512,1024]{1,0:T(8,128)(2,1)}, u32[]{:S(2)}) copy-start(bf16[512,1024]{1,0:T(8,128)(2,1)} %param.13) | copy-start | bytes 3145732
  9.6 32.9 %all-to-all-start.1 = ((bf16[8,64,1024]{2,1,0:T(8,128)(2,1)}), bf16[8,64,1024]{2,1,0:T(8,128)(2,1)S(1)}, u32[]{:S(2)}, u32[]{:S(2)}) async-start(bf16[8,64,1024]{2,1,0:T(8,128)(2,1)} %gather_fusion.3), calls=%async_computation.1 | async-start | bytes 2097152 | tf_op jit(solution)/shard_map/all_to_all | solution.py:89
  16.0 71.2 %all-gather.5.cloned.1.call-start = ((), (), s32[]{:S(2)}) async-start(), calls=%async_computation.3 | async-start | bytes 3932160 | tf_op jit(solution)/shard_map/all_gather | solution.py:97
  44.1 109.5 %all-gather.3.cloned.1.call-start = ((), (), s32[]{:S(2)}) async-start(), calls=%async_computation.2 | async-start | bytes 7077888 | tf_op jit(solution)/shard_map/all_gather | solution.py:95
  73.8 4.6 %copy-start.4 = (bf16[2,256,256]{2,1,0:T(8,128)(2,1)S(1)}, bf16[2,256,256]{2,1,0:T(8,128)(2,1)}, u32[]{:S(2)}) copy-start(bf16[2,256,256]{2,1,0:T(8,128)(2,1)} %param.16) | copy-start | bytes 786436
  73.8 4.6 %copy-start.7 = (bf16[2,256,256]{2,1,0:T(8,128)(2,1)S(1)}, bf16[2,256,256]{2,1,0:T(8,128)(2,1)}, u32[]{:S(2)}) copy-start(bf16[2,256,256]{2,1,0:T(8,128)(2,1)} %param.19) | copy-start | bytes 786436
  75.4 3.4 %copy-start.5 = (bf16[2,256,256]{2,1,0:T(8,128)(2,1)S(1)}, bf16[2,256,256]{2,1,0:T(8,128)(2,1)}, u32[]{:S(2)}) copy-start(bf16[2,256,256]{2,1,0:T(8,128)(2,1)} %param.17) | copy-start | bytes 786436
  75.4 3.4 %copy-start.6 = (bf16[2,256,256]{2,1,0:T(8,128)(2,1)S(1)}, bf16[2,256,256]{2,1,0:T(8,128)(2,1)}, u32[]{:S(2)}) copy-start(bf16[2,256,256]{2,1,0:T(8,128)(2,1)} %param.18) | copy-start | bytes 786436
  160.4 1.7 copy-start.2
  229.5 3.0 %copy-start.1 = (bf16[512,1024]{1,0:T(8,128)(2,1)S(1)}, bf16[512,1024]{1,0:T(8,128)(2,1)}, u32[]{:S(2)}) copy-start(bf16[512,1024]{1,0:T(8,128)(2,1)} %param.14) | copy-start | bytes 3145732
Sparse Core Ops, SparseCore 0:
  44.2 42.8 all-gather.4
  88.8 64.7 all-gather.2
where the time goes:
time: 240 us; the launch traced here: 239 us
  waiting for transfers between devices  93.2 us (39%)
  local copies, waits for them, and re-layouts  54.9 us (23%)
  matrix products  31.5 us (13%)
  blocking collectives  29 us (12%)
  between operations  13.7 us (6%)
  other arithmetic  10.6 us (4%)
  starting transfers between devices  6.4 us (3%)
    all_gather x1, waiting for transfers between devices, local(): lax.all_gather(own_x, 'col', axis=0, tiled=True)  59.1 us
    all_to_all x1, blocking collectives, local(): lax.all_to_all(held_x[send_slots], 'col', split_axis=0, concat_axis=0, ti...  29 us
    all_to_all x1, waiting for transfers between devices, local(): lax.all_to_all(held_y[send_slots], 'col', split_axis=0, concat_axis=0, ti...  26.5 us
    dot_general x4, matrix products, one_slot(): jnp.einsum('jbp,jqp->bjq', picked, stacked, preferred_element_type=jnp.fl...  20.2 us
    gather x4, local copies, waits for them, and re-layouts, one_slot(): picked = lower_blocks[pattern_rows]  14.1 us
    concatenate x1, local copies, waits for them, and re-layouts, join_panels(): jnp.concatenate([left_part[:, :PANEL], right_part[:, :PANEL], left_part[:...  8.62 us
    dot_general x1, matrix products, form_rows(): jnp.dot(remainder, real_form(inv_second), preferred_element_type=jnp.floa...  8.11 us
    all_gather x1, waiting for transfers between devices, local(): lax.all_gather(own_y, 'row', axis=0, tiled=True)  7.5 us
  transfers between devices with their start and end apart: 3, of which 3 were waited for; matrix products, arithmetic and copies ran while one was open for 6% of the time, Pallas kernels for 0%

commit v1 on v0

--- a/solution.py
+++ b/solution.py
@@ -91,9 +91,30 @@
     sources = lax.dynamic_index_in_dim(owner_grid, my_col, 0, keepdims=False)
     own_x = got_x[sources].reshape(PER * BS, row_width)
     own_y = got_y[sources].reshape(PER * BS, row_width)
-    lower_rows = form_rows(
-        lax.all_gather(own_x, "col", axis=0, tiled=True), inv_first, inv_second, couple_right
-    )
+
+    def corner_register(payload):
+        next_value = lax.axis_index("col")
+        tile_out = lax.axis_size("col")
+        piece_next, tmp, raw_out = (tile_out, next_value, payload.shape[0])
+        rows = tuple((it * piece_next if dev == 0 else it for dev, it in enumerate(payload.shape)))
+        state_next = jnp.zeros(rows, payload.dtype)
+        u1 = lax.dynamic_update_slice_in_dim(state_next, payload, tmp * raw_out, axis=0)
+        block_last = opened = payload
+        for m in [*range(1, piece_next // 2 + 1)]:
+            piece_out = tuple(((dev, (dev + 1) % piece_next) for dev in range(piece_next)))
+            block_last = lax.ppermute(block_last, "col", piece_out)
+            u1 = lax.dynamic_update_slice_in_dim(
+                u1, block_last, (tmp - m) % piece_next * raw_out, axis=0
+            )
+            if 2 * m < piece_next:
+                block_next = tuple(((dev, (dev - 1) % piece_next) for dev in range(piece_next)))
+                opened = lax.ppermute(opened, "col", block_next)
+                u1 = lax.dynamic_update_slice_in_dim(
+                    u1, opened, (tmp + m) % piece_next * raw_out, axis=0
+                )
+        return u1
+
+    lower_rows = form_rows(corner_register(own_x), inv_first, inv_second, couple_right)
     upper_rows = form_cols(lax.all_gather(own_y, "row", axis=0, tiled=True), inv_first, couple_left)
     stacked = stack_cols(upper_rows)
     column_count = stacked.shape[0]

time: 240 us -> 221 us (0.921)
  the two profiles are of different devices: /device:TPU:0 before, /device:TPU:11 now
where the time goes in v1:
time: 221 us; the launch traced here: 219 us
  waiting for transfers between devices  81.9 us (37%)
  local copies, waits for them, and re-layouts  58.6 us (27%)
  matrix products  30.8 us (14%)
  starting transfers between devices  20 us (9%)
  other arithmetic  14 us (6%)
  between operations  13.7 us (6%)
    ppermute x3, waiting for transfers between devices, corner_register(): opened = lax.ppermute(opened, 'col', block_next)  58.9 us
    all_to_all x1, waiting for transfers between devices, local(): lax.all_to_all(held_x[send_slots], 'col', split_axis=0, concat_axis=0, ti...  23 us
    dot_general x4, matrix products, one_slot(): jnp.einsum('jbp,jqp->bjq', picked, stacked, preferred_element_type=jnp.fl...  20.2 us
    gather x4, local copies, waits for them, and re-layouts, one_slot(): picked = lower_blocks[pattern_rows]  14.1 us
    concatenate x1, local copies, waits for them, and re-layouts, join_panels(): jnp.concatenate([left_part[:, :PANEL], right_part[:, :PANEL], left_part[:...  8.63 us
    dot_general x1, matrix products, form_rows(): jnp.dot(remainder, real_form(inv_second), preferred_element_type=jnp.floa...  7.39 us
    ppermute x4, starting transfers between devices, corner_register(): block_last = lax.ppermute(block_last, 'col', piece_out)  7.19 us
    all_to_all x1, starting transfers between devices, local(): lax.all_to_all(held_y[send_slots], 'col', split_axis=0, concat_axis=0, ti...  6.79 us
  transfers between devices with their start and end apart: 10, of which 4 were waited for; matrix products, arithmetic and copies ran while one was open for 19% of the time, Pallas kernels for 0%

profile of v1, /device:TPU:11, one launch (start us, length us, event | category | flops | bytes accessed | tf_op | source)
XLA Modules:
  0.0 219.2 jit_solution(12466023344631983052)
XLA Ops:
  8.1 1.6 gather_fusion.1
  9.7 5.6 %all-to-all-start = ((bf16[8,64,1024]{2,1,0:T(8,128)(2,1)}), bf16[8,64,1024]{2,1,0:T(8,128)(2,1)S(1)}, u32[]{:S(2)}, u32[]{:S(2)}) async-start(bf16[8,64,1024]{2,1,0:T(8,128)(2,1)} %gather_fusion.1), calls=%async_computation | async-start | bytes 2097152 | tf_op jit(solution)/shard_map/all_to_all | solution.py:88
  15.3 23.0 %all-to-all-done = bf16[8,64,1024]{2,1,0:T(8,128)(2,1)S(1)} async-done(((bf16[8,64,1024]{2,1,0:T(8,128)(2,1)}), bf16[8,64,1024]{2,1,0:T(8,128)(2,1)S(1)}, u32[]{:S(2)}, u32[]{:S(2)}) %all-to-all-start) | async-done | bytes 1048608 | tf_op jit(solution)/shard_map/all_to_all | solution.py:88
  39.0 1.8 collective-permute-start
  40.7 1.6 gather_fusion.3
  42.4 6.8 %all-to-all-start.1 = ((bf16[8,64,1024]{2,1,0:T(8,128)(2,1)}), bf16[8,64,1024]{2,1,0:T(8,128)(2,1)S(1)}, u32[]{:S(2)}, u32[]{:S(2)}) async-start(bf16[8,64,1024]{2,1,0:T(8,128)(2,1)} %gather_fusion.3), calls=%async_computation.1 | async-start | bytes 2097152 | tf_op jit(solution)/shard_map/all_to_all | solution.py:89
  50.5 1.7 collective-permute-start.2
  53.2 1.0 slice_bitcast_fusion.3
  54.5 39.0 %collective-permute-done.1 = bf16[384,1024]{1,0:T(8,128)(2,1)} collective-permute-done((bf16[384,1024]{1,0:T(8,128)(2,1)S(1)}, bf16[384,1024]{1,0:T(8,128)(2,1)}, u32[]{:S(2)}, u32[]{:S(2)}) %collective-permute-start.1) | collective-permute-done | bytes 786464 | tf_op jit(solution)/shard_map/ppermute | solution.py:111
  94.2 1.5 copy.18
  95.7 1.7 collective-permute-start.4
  98.3 1.7 fusion.58
  100.0 1.9 slice_bitcast_fusion.4
  101.9 1.5 gather_fusion.4
  103.4 8.8 %collective-permute-done.3 = bf16[384,1024]{1,0:T(8,128)(2,1)} collective-permute-done((bf16[384,1024]{1,0:T(8,128)(2,1)}, bf16[384,1024]{1,0:T(8,128)(2,1)}, u32[]{:S(2)}, u32[]{:S(2)}) %collective-permute-start.3) | collective-permute-done | bytes 786464 | tf_op jit(solution)/shard_map/ppermute | solution.py:111
  113.2 2.0 collective-permute-start.6
  115.1 1.2 constant_dynamic-update-slice_fusion.6
  116.3 1.2 constant_dynamic-update-slice_fusion.5
  117.5 1.2 constant_dynamic-update-slice_fusion.4
  118.7 1.2 constant_dynamic-update-slice_fusion.3
  120.0 11.1 %collective-permute-done.5 = bf16[384,1024]{1,0:T(8,128)(2,1)S(1)} collective-permute-done((bf16[384,1024]{1,0:T(8,128)(2,1)}, bf16[384,1024]{1,0:T(8,128)(2,1)S(1)}, u32[]{:S(2)}, u32[]{:S(2)}) %collective-permute-start.5) | collective-permute-done | bytes 786464 | tf_op jit(solution)/shard_map/ppermute | solution.py:111
  131.2 2.1 fusion.61
  133.3 1.9 convolution_convert_fusion.1
  135.2 7.4 %convolution_convert_fusion = bf16[3072,512]{0,1:T(8,128)(2,1)} fusion(bf16[3072,256]{1,0:T(8,128)(2,1)} %get-tuple-element.63, bf16[3072,256]{1,0:T(8,128)(2,1)} %get-tuple-element.64, bf16[3072,512]{0,1:T(8,128)(2,1)S(1)} %convolution_convert_fusion.1, bf16[256,256]{1,0:T(8,128)(2,1)} %get-tuple-element.86, bf16[256,256]{1,0:T(8,128)(2,1)} %get-tuple-element.88, ...), kind=kOutput, calls=%fused_computation.20 | convolution fusion | flops 3236429824 | bytes 10223616 | tf_op jit(solution)/shard_map/dot_general | solution.py:39
  142.8 1.7 copy-done.2
  144.7 3.1 %pad_maximum_fusion = bf16[3072,1024]{0,1:T(8,128)(2,1)} fusion(bf16[3072,256]{0,1:T(8,128)(2,1)S(1)} %get-tuple-element.73, bf16[3072,256]{0,1:T(8,128)(2,1)S(1)} %get-tuple-element.71, bf16[3072,256]{0,1:T(8,128)(2,1)S(1)} %get-tuple-element.72, bf16[3072,256]{0,1:T(8,128)(2,1)S(1)} %get-tuple-element.70), kind=kLoop, calls=%fused_computation.17 | loop fusion | flops 25165824 | bytes 12582912 | tf_op jit(solution)/shard_map/concatenate | solution.py:24
  147.8 8.6 %copy.12 = bf16[3072,1024]{1,0:T(8,128)(2,1)} copy(bf16[3072,1024]{0,1:T(8,128)(2,1)} %pad_maximum_fusion) | data formatting | bytes 12582912 | tf_op jit(solution)/shard_map/concatenate | solution.py:24
  156.5 2.1 fusion.62
  158.6 1.0 fusion.11
  160.7 3.2 %pad_maximum_fusion.1 = bf16[24,128,1024]{2,1,0:T(8,128)(2,1)} fusion(bf16[24,64,1024]{2,1,0:T(8,128)(2,1)S(1)} %bitcast.99, bf16[24,64,512]{2,1,0:T(8,128)(2,1)S(1)} %maximum_negate_fusion, bf16[24,64,512]{2,1,0:T(8,128)(2,1)S(1)} %bitcast.103), kind=kLoop, calls=%fused_computation.18 | loop fusion | flops 18874368 | bytes 12582912 | tf_op jit(solution)/shard_map/concatenate | solution.py:65
  163.9 45.5 %while.10 = (s32[]{:T(128)}, bf16[4,64,24,128]{3,2,1,0:T(8,128)(2,1)}, bf16[4,64,24,128]{3,2,1,0:T(8,128)(2,1)}, s32[4,24]{1,0:T(4,128)}, bf16[48,64,1024]{2,1,0...) while((s32[]{:T(128)}, bf16[4,64,24,128]{3,2,1,0:T(8,128)(2,1)}, ...), condition=%wide.region_4.5_spmd, body=%wide.region_3.4_spmd.sunk | while | flops 403244096 | bytes 18093012 | solution.py:130
  164.6 3.5 %gather_fusion = bf16[24,64,1024]{2,1,0:T(8,128)(2,1)S(1)} fusion(bf16[48,64,1024]{2,1,0:T(8,128)(2,1)} %get-tuple-element.145, s32[1024]{0:T(1024)S(1)} %pad_clamp_fusion.4), kind=kCustom, calls=%fused_computation.clone.1 | custom fusion | bytes 6291552 | tf_op jit(solution)/shard_map/while/body/eval_jaxpr/gather | solution.py:126
  168.1 1.0 constant_dynamic-slice_fusion.4
  169.2 5.1 %fusion.76 = bf16[1,64,24,128]{3,1,2,0:T(8,128)(2,1)S(1)} fusion(bf16[24,64,1024]{2,1,0:T(8,128)(2,1)S(1)} %gather_fusion, bf16[24,128,1024]{2,1,0:T(8,128)(2,1)} %get-tuple-element.146, bf16[1,64,24,128]{3,2,1,0:T(8,128)(2,1)S(1)} %constant_dynamic-slice_fusion.4), kind=kOutput, calls=%fused_computation.8.clone.1 | convolution fusion | flops 403243008 | bytes 10223616 | tf_op jit(solution)/shard_map/while/body/eval_jaxpr/jbp,jqp->bjq/dot_general | solution.py:127
  174.3 1.0 copy_dynamic-update-slice_fusion.2
  176.0 3.5 %gather_fusion = bf16[24,64,1024]{2,1,0:T(8,128)(2,1)S(1)} fusion(bf16[48,64,1024]{2,1,0:T(8,128)(2,1)} %get-tuple-element.145, s32[1024]{0:T(1024)S(1)} %pad_clamp_fusion.4), kind=kCustom, calls=%fused_computation.clone.1 | custom fusion | bytes 6291552 | tf_op jit(solution)/shard_map/while/body/eval_jaxpr/gather | solution.py:126
  179.5 1.0 constant_dynamic-slice_fusion.4
  180.6 5.1 %fusion.76 = bf16[1,64,24,128]{3,1,2,0:T(8,128)(2,1)S(1)} fusion(bf16[24,64,1024]{2,1,0:T(8,128)(2,1)S(1)} %gather_fusion, bf16[24,128,1024]{2,1,0:T(8,128)(2,1)} %get-tuple-element.146, bf16[1,64,24,128]{3,2,1,0:T(8,128)(2,1)S(1)} %constant_dynamic-slice_fusion.4), kind=kOutput, calls=%fused_computation.8.clone.1 | convolution fusion | flops 403243008 | bytes 10223616 | tf_op jit(solution)/shard_map/while/body/eval_jaxpr/jbp,jqp->bjq/dot_general | solution.py:127
  185.6 1.0 copy_dynamic-update-slice_fusion.2
  187.4 3.5 %gather_fusion = bf16[24,64,1024]{2,1,0:T(8,128)(2,1)S(1)} fusion(bf16[48,64,1024]{2,1,0:T(8,128)(2,1)} %get-tuple-element.145, s32[1024]{0:T(1024)S(1)} %pad_clamp_fusion.4), kind=kCustom, calls=%fused_computation.clone.1 | custom fusion | bytes 6291552 | tf_op jit(solution)/shard_map/while/body/eval_jaxpr/gather | solution.py:126
  190.9 1.0 constant_dynamic-slice_fusion.4
  191.9 5.1 %fusion.76 = bf16[1,64,24,128]{3,1,2,0:T(8,128)(2,1)S(1)} fusion(bf16[24,64,1024]{2,1,0:T(8,128)(2,1)S(1)} %gather_fusion, bf16[24,128,1024]{2,1,0:T(8,128)(2,1)} %get-tuple-element.146, bf16[1,64,24,128]{3,2,1,0:T(8,128)(2,1)S(1)} %constant_dynamic-slice_fusion.4), kind=kOutput, calls=%fused_computation.8.clone.1 | convolution fusion | flops 403243008 | bytes 10223616 | tf_op jit(solution)/shard_map/while/body/eval_jaxpr/jbp,jqp->bjq/dot_general | solution.py:127
  197.0 1.0 copy_dynamic-update-slice_fusion.2
  198.7 3.5 %gather_fusion = bf16[24,64,1024]{2,1,0:T(8,128)(2,1)S(1)} fusion(bf16[48,64,1024]{2,1,0:T(8,128)(2,1)} %get-tuple-element.145, s32[1024]{0:T(1024)S(1)} %pad_clamp_fusion.4), kind=kCustom, calls=%fused_computation.clone.1 | custom fusion | bytes 6291552 | tf_op jit(solution)/shard_map/while/body/eval_jaxpr/gather | solution.py:126
  202.2 1.0 constant_dynamic-slice_fusion.4
  203.3 5.1 %fusion.76 = bf16[1,64,24,128]{3,1,2,0:T(8,128)(2,1)S(1)} fusion(bf16[24,64,1024]{2,1,0:T(8,128)(2,1)S(1)} %gather_fusion, bf16[24,128,1024]{2,1,0:T(8,128)(2,1)} %get-tuple-element.146, bf16[1,64,24,128]{3,2,1,0:T(8,128)(2,1)S(1)} %constant_dynamic-slice_fusion.4), kind=kOutput, calls=%fused_computation.8.clone.1 | convolution fusion | flops 403243008 | bytes 10223616 | tf_op jit(solution)/shard_map/while/body/eval_jaxpr/jbp,jqp->bjq/dot_general | solution.py:127
  208.4 1.0 copy_dynamic-update-slice_fusion.2
  209.4 3.0 %copy.25 = bf16[32,8,24,128]{3,1,2,0:T(8,128)(2,1)} copy(bf16[32,8,24,128]{3,2,1,0:T(8,128)(2,1)} %bitcast.33) | data formatting | bytes 3145728
  (71 shorter events, 11.7 us)
Async XLA Ops:
  6.5 1.5 copy-start
  6.5 34.2 %copy-start.4 = (bf16[512,1024]{1,0:T(8,128)(2,1)S(1)}, bf16[512,1024]{1,0:T(8,128)(2,1)}, u32[]{:S(2)}) copy-start(bf16[512,1024]{1,0:T(8,128)(2,1)} %param.14) | copy-start | bytes 3145732
  9.7 28.7 %all-to-all-start = ((bf16[8,64,1024]{2,1,0:T(8,128)(2,1)}), bf16[8,64,1024]{2,1,0:T(8,128)(2,1)S(1)}, u32[]{:S(2)}, u32[]{:S(2)}) async-start(bf16[8,64,1024]{2,1,0:T(8,128)(2,1)} %gather_fusion.1), calls=%async_computation | async-start | bytes 2097152 | tf_op jit(solution)/shard_map/all_to_all | solution.py:88
  39.0 11.6 %collective-permute-start = (bf16[384,1024]{1,0:T(8,128)(2,1)S(1)}, bf16[384,1024]{1,0:T(8,128)(2,1)}, u32[]{:S(2)}, u32[]{:S(2)}) collective-permute-start(bf16[384,1024]{1,0:T(8,128)(2,1)S(1)} %bitcast.104), channel_id=1, source_target_pairs={{0,1},{1,2},{2,3},{3,4},{4,5},{5,6},{6,7},{7,0},{8,9},{9,10},{10,1... | collective-permute-start | bytes 2359304 | tf_op jit(solution)/shard_map/ppermute | solution.py:105
  42.4 51.8 %copy-start.3 = (bf16[256,3072]{1,0:T(8,128)(2,1)S(1)}, bf16[256,3072]{1,0:T(8,128)(2,1)}, u32[]{:S(2)}) copy-start(bf16[256,3072]{1,0:T(8,128)(2,1)} %param.11) | copy-start | bytes 4718596
  42.4 59.5 %all-to-all-start.1 = ((bf16[8,64,1024]{2,1,0:T(8,128)(2,1)}), bf16[8,64,1024]{2,1,0:T(8,128)(2,1)S(1)}, u32[]{:S(2)}, u32[]{:S(2)}) async-start(bf16[8,64,1024]{2,1,0:T(8,128)(2,1)} %gather_fusion.3), calls=%async_computation.1 | async-start | bytes 2097152 | tf_op jit(solution)/shard_map/all_to_all | solution.py:89
  49.1 107.3 %all-gather.2.cloned.1.call-start = ((), (), s32[]{:S(2)}) async-start(), calls=%async_computation.2 | async-start | bytes 3932160 | tf_op jit(solution)/shard_map/all_gather | solution.py:118
  49.1 44.3 %collective-permute-start.1 = (bf16[384,1024]{1,0:T(8,128)(2,1)S(1)}, bf16[384,1024]{1,0:T(8,128)(2,1)}, u32[]{:S(2)}, u32[]{:S(2)}) collective-permute-start(bf16[384,1024]{1,0:T(8,128)(2,1)S(1)} %bitcast.105), channel_id=1, source_target_pairs={{0,7},{1,0},{2,1},{3,2},{4,3},{5,4},{6,5},{7,6},{8,15},{9,8},{10,9... | collective-permute-start | bytes 2359304 | tf_op jit(solution)/shard_map/ppermute | solution.py:111
  50.5 42.9 %copy-start.8 = (bf16[256,256]{1,0:T(8,128)(2,1)}, bf16[256,256]{1,0:T(8,128)(2,1)S(1)}, u32[]{:S(2)}) copy-start(bf16[256,256]{1,0:T(8,128)(2,1)S(1)} %get-tuple-element.84) | copy-start | bytes 393220
  50.5 42.9 %copy-start.10 = (bf16[256,256]{1,0:T(8,128)(2,1)}, bf16[256,256]{1,0:T(8,128)(2,1)S(1)}, u32[]{:S(2)}) copy-start(bf16[256,256]{1,0:T(8,128)(2,1)S(1)} %get-tuple-element.85) | copy-start | bytes 393220
  50.5 45.1 %collective-permute-start.2 = (bf16[384,1024]{1,0:T(8,128)(2,1)}, bf16[384,1024]{1,0:T(8,128)(2,1)}, u32[]{:S(2)}, u32[]{:S(2)}) collective-permute-start(bf16[384,1024]{1,0:T(8,128)(2,1)} %collective-permute-done), channel_id=1, source_target_pairs={{0,1},{1,2},{2,3},{3,4},{4,5},{5,6},{6,7},{7,0},{8,9},{9,10},{10,1... | collective-permute-start | bytes 2359304 | tf_op jit(solution)/shard_map/ppermute | solution.py:105
  54.5 39.0 %copy-start.5 = (bf16[256,512]{1,0:T(8,128)(2,1)}, bf16[256,512]{1,0:T(8,128)(2,1)S(1)}, u32[]{:S(2)}) copy-start(bf16[256,512]{1,0:T(8,128)(2,1)S(1)} %convolution_convert_fusion.2) | copy-start | bytes 786436
  93.4 18.8 %collective-permute-start.3 = (bf16[384,1024]{1,0:T(8,128)(2,1)}, bf16[384,1024]{1,0:T(8,128)(2,1)}, u32[]{:S(2)}, u32[]{:S(2)}) collective-permute-start(bf16[384,1024]{1,0:T(8,128)(2,1)} %collective-permute-done.1), channel_id=1, source_target_pairs={{0,7},{1,0},{2,1},{3,2},{4,3},{5,4},{6,5},{7,6},{8,15},{9,8},{10,9... | collective-permute-start | bytes 2359304 | tf_op jit(solution)/shard_map/ppermute | solution.py:111
  95.7 17.5 %collective-permute-start.4 = (bf16[384,1024]{1,0:T(8,128)(2,1)}, bf16[384,1024]{1,0:T(8,128)(2,1)S(1)}, u32[]{:S(2)}, u32[]{:S(2)}) collective-permute-start(bf16[384,1024]{1,0:T(8,128)(2,1)} %collective-permute-done.2), channel_id=1, source_target_pairs={{0,1},{1,2},{2,3},{3,4},{4,5},{5,6},{6,7},{7,0},{8,9},{9,10},{10,1... | collective-permute-start | bytes 2359304 | tf_op jit(solution)/shard_map/ppermute | solution.py:105
  112.3 18.8 %collective-permute-start.5 = (bf16[384,1024]{1,0:T(8,128)(2,1)}, bf16[384,1024]{1,0:T(8,128)(2,1)S(1)}, u32[]{:S(2)}, u32[]{:S(2)}) collective-permute-start(bf16[384,1024]{1,0:T(8,128)(2,1)} %collective-permute-done.3), channel_id=1, source_target_pairs={{0,7},{1,0},{2,1},{3,2},{4,3},{5,4},{6,5},{7,6},{8,15},{9,8},{10,9... | collective-permute-start | bytes 2359304 | tf_op jit(solution)/shard_map/ppermute | solution.py:111
  113.2 18.0 %collective-permute-start.6 = (bf16[384,1024]{1,0:T(8,128)(2,1)S(1)}, bf16[384,1024]{1,0:T(8,128)(2,1)S(1)}, u32[]{:S(2)}, u32[]{:S(2)}) collective-permute-start(bf16[384,1024]{1,0:T(8,128)(2,1)S(1)} %collective-permute-done.4), channel_id=1, source_target_pairs={{0,1},{1,2},{2,3},{3,4},{4,5},{5,6},{6,7},{7,0},{8,9},{9,10},{10,1... | collective-permute-start | bytes 2359304 | tf_op jit(solution)/shard_map/ppermute | solution.py:105
  131.2 2.1 copy-start.9
  131.2 2.1 copy-start.11
  142.6 1.9 copy-start.2
  156.5 2.1 copy-start.6
  156.5 2.1 copy-start.7
  209.4 3.0 %copy-start.1 = (bf16[512,1024]{1,0:T(8,128)(2,1)S(1)}, bf16[512,1024]{1,0:T(8,128)(2,1)}, u32[]{:S(2)}) copy-start(bf16[512,1024]{1,0:T(8,128)(2,1)} %param.13) | copy-start | bytes 3145732
Sparse Core Ops, SparseCore 0:
  103.6 42.5 all-gather.1
